TPU v7x, 512 devices: a whole 4x8x8 slice. The times are simulated.
512 devices in a mesh: dp: 32 (over y, x), ctx: 16 (over z, core).
Axes of the slice: x: 4, y: 8, z: 8, core: 2. Of those that a mesh axis runs over, the one named last changes fastest.
Arguments:
- queries: bfloat16 [32, 2048, 1024], P('dp', 'ctx'), may hold values from -6 to 6
- key_rows: bfloat16 [32, 2048, 128], P('dp', 'ctx'), may hold values from -6 to 6
- x_rows: bfloat16 [32, 2048, 4096], P('dp', 'ctx'), may hold values from -6 to 6
- value_weight: bfloat16 [4096, 128], replicated, may hold values from -0.09375 to 0.09375
- grad_context: bfloat16 [32, 2048, 1024], P('dp', 'ctx'), may hold values from -6 to 6
- doc_lengths: int32 [32, 8], P('dp'), may hold values from 1 to 1024, 2048 in all within a row
- block_order: int32 [32, 16], P('dp'), may hold values from 0 to 15, each once within a row
Outputs:
- context: bfloat16 [32, 2048, 1024], P('dp', 'ctx')
- grad_queries: bfloat16 [32, 2048, 1024], P('dp', 'ctx')
- grad_keys: bfloat16 [32, 2048, 128], P('dp', 'ctx')
- grad_values: bfloat16 [32, 2048, 128], P('dp', 'ctx')
- grad_weight: float32 [4096, 128], P(('dp', 'ctx'))
Inputs may be any that keep to these rules, and one draw needn't show every extreme that they name: `doc_lengths`: each row is the document lengths of one microbatch in order, summing to 2048; the longest is exactly 1024. `block_order`: each row is a permutation of the 16 sequence blocks.
All inputs are finite; a program needn't handle non-finite values.
Results may differ from a plain program's by a relative error of at most 0.019.
Values may be sent and summed in bfloat16 or wider, within the bound.
A program may use at most 64 MiB of HBM per device.

v0:
```python
import math

import jax
import jax.numpy as jnp
from jax import lax
from jax.sharding import PartitionSpec as P

BLOCK = 128


def doc_ids(lengths, positions):
    ends = jnp.cumsum(lengths)
    return jnp.sum((positions[:, None] >= ends[None, :]).astype(jnp.int32), axis=1)


def body(queries, key_rows, x_rows, value_weight, grad_context, doc_lengths, block_order):
    head_dim = key_rows.shape[2]
    row_count = queries.shape[1]
    head_count = queries.shape[2] // head_dim
    group_size = min(4, head_count)
    group_count = head_count // group_size
    score_scale = 1.0 / math.sqrt(head_dim)
    input_local = x_rows[0]
    value_rows = jnp.dot(input_local, value_weight, preferred_element_type=jnp.float32).astype(
        jnp.bfloat16
    )
    local_pairs = jnp.concatenate([key_rows[0], value_rows], axis=1)
    all_pairs = lax.all_gather(local_pairs, "ctx", axis=0, tiled=True)
    seq_len = all_pairs.shape[0]
    key_all = all_pairs[:, :head_dim]
    value_all = all_pairs[:, head_dim:]
    owned_count = row_count // BLOCK
    owned_blocks = lax.dynamic_slice_in_dim(
        block_order[0], lax.axis_index("ctx") * owned_count, owned_count
    )
    offsets = jnp.arange(BLOCK, dtype=jnp.int32)
    query_pos = (owned_blocks[:, None] * BLOCK + offsets[None, :]).reshape(row_count)
    key_pos = jnp.arange(seq_len, dtype=jnp.int32)
    lengths = doc_lengths[0]
    allowed = (doc_ids(lengths, query_pos)[:, None] == doc_ids(lengths, key_pos)[None, :]) & (
        key_pos[None, :] <= query_pos[:, None]
    )
    mask_rows = jnp.tile(allowed, (group_size, 1))
    query_groups = (
        queries[0]
        .reshape(row_count, group_count, group_size, head_dim)
        .transpose(1, 2, 0, 3)
        .reshape(group_count, group_size * row_count, head_dim)
    )
    grad_groups = (
        grad_context[0]
        .reshape(row_count, group_count, group_size, head_dim)
        .transpose(1, 2, 0, 3)
        .reshape(group_count, group_size * row_count, head_dim)
    )

    def attend(pieces):
        query_group, grad_group = pieces
        scores = jnp.dot(query_group, key_all.T, preferred_element_type=jnp.float32) * score_scale
        scores = jnp.where(mask_rows, scores, -jnp.inf)
        row_max = jnp.max(scores, axis=1, keepdims=True)
        exp_scores = jnp.exp(scores - row_max)
        prob = exp_scores / jnp.sum(exp_scores, axis=1, keepdims=True)
        weights = prob.astype(jnp.bfloat16)
        context = jnp.dot(weights, value_all, preferred_element_type=jnp.float32).astype(
            jnp.bfloat16
        )
        delta = jnp.sum(
            grad_group.astype(jnp.float32) * context.astype(jnp.float32), axis=1, keepdims=True
        )
        grad_prob = jnp.dot(grad_group, value_all.T, preferred_element_type=jnp.float32)
        grad_scores = (prob * (grad_prob - delta) * score_scale).astype(jnp.bfloat16)
        grad_query = jnp.dot(grad_scores, key_all, preferred_element_type=jnp.float32).astype(
            jnp.bfloat16
        )
        contract = (((0,), (0,)), ((), ()))
        key_part = lax.dot_general(
            grad_scores, query_group, contract, preferred_element_type=jnp.float32
        )
        value_part = lax.dot_general(
            weights, grad_group, contract, preferred_element_type=jnp.float32
        )
        return (context, grad_query, key_part, value_part)

    context_groups, grad_query_groups, key_parts, value_parts = lax.map(
        attend, (query_groups, grad_groups)
    )
    partial_grads = jnp.concatenate(
        [jnp.sum(key_parts, axis=0), jnp.sum(value_parts, axis=0)], axis=1
    )
    summed_grads = lax.psum_scatter(
        partial_grads.astype(jnp.bfloat16), "ctx", scatter_dimension=0, tiled=True
    ).astype(jnp.float32)
    grad_keys = summed_grads[:, :head_dim].astype(jnp.bfloat16)
    grad_values = summed_grads[:, head_dim:].astype(jnp.bfloat16)

    def restore(grouped):
        return (
            grouped.reshape(group_count, group_size, row_count, head_dim)
            .transpose(2, 0, 1, 3)
            .reshape(row_count, head_count * head_dim)
        )

    context = restore(context_groups)
    grad_queries = restore(grad_query_groups)
    grad_weight = lax.psum_scatter(
        lax.dot_general(
            input_local, grad_values, (((0,), (0,)), ((), ())), preferred_element_type=jnp.float32
        ),
        ("dp", "ctx"),
        scatter_dimension=0,
        tiled=True,
    )
    return (context[None], grad_queries[None], grad_keys[None], grad_values[None], grad_weight)


def solution(mesh):
    placed = (
        P("dp", "ctx", None),
        P("dp", "ctx", None),
        P("dp", "ctx", None),
        P(),
        P("dp", "ctx", None),
        P("dp", None),
        P("dp", None),
    )
    return jax.shard_map(
        body,
        mesh=mesh,
        in_specs=placed,
        out_specs=(
            P("dp", "ctx", None),
            P("dp", "ctx", None),
            P("dp", "ctx", None),
            P("dp", "ctx", None),
            P(("dp", "ctx"), None),
        ),
        check_vma=False,
    )
```

profile of v0, /device:TPU:1, one launch (start us, length us, event | category | flops | bytes accessed | tf_op | source)
XLA Modules:
  0.0 433.9 jit_solution(4083681770786811816)
XLA Ops:
  7.2 0.9 copy.31
  8.4 1.7 convolution_convert_fusion.2
  10.9 0.8 reduce-window.8
  11.7 1.1 reshape_squeeze.7
  13.2 1.1 reshape_squeeze.6
  16.3 41.6 %all-gather.2.cloned.1.call-done = bf16[2048,256]{0,1:T(8,128)(2,1)} async-done(((bf16[128,256]{0,1:T(8,128)(2,1)}), bf16[2048,256]{0,1:T(8,128)(2,1)}) %all-gather.2.cloned.1.call-update) | async-done | bytes 1048592 | tf_op jit(solution)/shard_map/all_gather | solution.py:28
  57.8 1.3 fusion.28
  59.6 19.1 %while.17 = (s32[]{:T(128)}, bf16[2,512,128]{1,2,0:T(8,128)(2,1)}, bf16[2,512,128]{2,1,0:T(8,128)(2,1)}, f32[2,2048,128]{2,1,0:T(8,128)}, f32[2,2048,128]{2,1,0:...) while((s32[]{:T(128)}, bf16[2,512,128]{1,2,0:T(8,128)(2,1)}, ...), condition=%wide.region_7.8_spmd.clone, body=%wide.region_3.7_spmd.clone.sunk | while | flops 1628830208 | bytes 79577432 | solution.py:85
  59.7 0.9 fusion.63
  60.6 1.2 fusion.64
  61.8 1.2 fusion.65
  63.0 0.8 bitcast_dynamic-update-slice_fusion.2
  63.9 0.9 multiply_convert_fusion.2
  65.5 0.8 fusion.67
  66.3 0.8 fusion.66
  67.9 1.3 copy-done.4
  69.2 0.9 fusion.63
  70.2 1.2 fusion.64
  71.4 1.2 fusion.65
  72.6 0.8 bitcast_dynamic-update-slice_fusion.2
  73.5 0.9 multiply_convert_fusion.2
  75.9 0.8 fusion.66
  77.5 1.3 copy-done.4
  78.8 1.7 reduce_sum.56
  80.5 1.8 reduce_sum.57
  82.3 1.1 pad_maximum_fusion
  83.5 56.4 %reduce-scatter.3.cloned.1.call-done = bf16[128,256]{1,0:T(8,128)(2,1)} async-done(((bf16[2048,256]{1,0:T(8,128)(2,1)}), bf16[128,256]{1,0:T(8,128)(2,1)}) %reduce-scatter.3.cloned.1.call-update) | async-done | bytes 65552 | tf_op jit(solution)/shard_map/reduce_scatter | solution.py:91
  139.9 2.6 convolution_bitcast_fusion.2
  142.8 0.9 broadcast_in_dim_reshape.8
  143.9 0.9 broadcast_in_dim_reshape.9
  145.4 280.4 %all-reduce.3.cloned.1.call-done = f32[4096,128]{0,1:T(8,128)} async-done(((f32[4096,128]{0,1:T(8,128)}), f32[4096,128]{0,1:T(8,128)}) %all-reduce.3.cloned.1.call-update) | async-done | bytes 2097168
  425.8 0.9 constant_dynamic-slice_fusion
  (71 shorter events, 9.4 us)
Async XLA Ops:
  7.2 1.2 copy-start
  7.2 7.2 %copy-start.12 = (s32[1,16]{1,0:T(1,128)S(1)}, s32[1,16]{1,0:T(1,128)}, u32[]{:S(2)}) copy-start(s32[1,16]{1,0:T(1,128)} %param.15) | copy-start | bytes 196
  7.2 50.6 %all-gather.2.cloned.1.call-start = ((), (), s32[]{:S(2)}) async-start(), calls=%async_computation.1 | async-start | bytes 1114112 | tf_op jit(solution)/shard_map/all_gather | solution.py:28
  10.8 129.1 %reduce-scatter.3.cloned.1.call-start = ((), (), s32[]{:S(2)}) async-start(), calls=%async_computation.2 | async-start | bytes 1114112 | tf_op jit(solution)/shard_map/reduce_scatter | solution.py:91
  61.8 1.2 copy-start.5
  63.8 2.5 copy-start.6
  63.9 1.7 copy-start.1
  64.9 1.5 copy-start.8
  65.5 1.6 copy-start.3
  66.3 1.6 copy-start.2
  67.1 2.1 copy-start.9
  67.9 1.3 copy-start.4
  71.4 1.2 copy-start.5
  73.4 2.5 copy-start.6
  73.4 1.7 copy-start.1
  74.4 1.5 copy-start.8
  75.1 1.6 copy-start.3
  75.9 1.6 copy-start.2
  76.7 2.1 copy-start.9
  77.5 1.3 copy-start.4
  82.3 60.2 %copy-start.7 = (bf16[2,512,128]{1,2,0:T(8,128)(2,1)S(1)}, bf16[2,512,128]{1,2,0:T(8,128)(2,1)}, u32[]{:S(2)}) copy-start(bf16[2,512,128]{1,2,0:T(8,128)(2,1)} %get-tuple-element.60) | copy-start | bytes 786436
  83.4 60.3 %copy-start.10 = (bf16[2,512,128]{2,1,0:T(8,128)(2,1)S(1)}, bf16[2,512,128]{2,1,0:T(8,128)(2,1)}, u32[]{:S(2)}) copy-start(bf16[2,512,128]{2,1,0:T(8,128)(2,1)} %get-tuple-element.61) | copy-start | bytes 786436
  83.4 342.4 %all-reduce.3.cloned.1.call-start = ((), (), s32[]{:S(2)}) async-start(), calls=%async_computation.3 | async-start | bytes 4194304
  139.9 4.9 %copy-start.11 = (bf16[128,256]{1,0:T(8,128)(2,1)S(1)}, bf16[128,256]{1,0:T(8,128)(2,1)}, u32[]{:S(2)}) copy-start(bf16[128,256]{1,0:T(8,128)(2,1)} %reduce-scatter.3.cloned.1.call-done) | copy-start | bytes 196612
Sparse Core Ops, SparseCore 0:
  10.9 46.8 all-gather.1
  83.6 56.3 reduce-scatter.2
  145.6 280.1 all-reduce.2
where the time goes:
time: 435 us; the launch traced here: 434 us
  waiting for transfers between devices  378 us (87%)
  matrix products  14.3 us (3%)
  local copies, waits for them, and re-layouts  14.1 us (3%)
  between operations  13.9 us (3%)
  other arithmetic  12.8 us (3%)
    unnamed x4, waiting for transfers between devices  280 us
    reduce_scatter x1, waiting for transfers between devices, body(): lax.psum_scatter(partial_grads.astype(jnp.bfloat16), 'ctx', scatter_dimen...  56.4 us
    all_gather x1, waiting for transfers between devices, body(): all_pairs = lax.all_gather(local_pairs, 'ctx', axis=0, tiled=True)  41.6 us
  transfers between devices with their start and end apart: 3, of which 3 were waited for; matrix products, arithmetic and copies ran while one was open for 2% of the time, Pallas kernels for 0%

commit v1 on v0

v1 whole, which is shorter than its diff:
```python
import functools
import math

import jax
import jax.numpy as jnp
from jax import lax
from jax.experimental import pallas as pl
from jax.experimental.pallas import tpu as pltpu
from jax.sharding import PartitionSpec as P

BLOCK = 128
MESH = pl.DeviceIdType.MESH
NEG = -1e30


def remote(src, dst, send_sem, recv_sem, device):
    return pltpu.make_async_remote_copy(
        src_ref=src,
        dst_ref=dst,
        send_sem=send_sem,
        recv_sem=recv_sem,
        device_id=device,
        device_id_type=MESH,
    )


def dot(a, b):
    return jnp.dot(a, b, preferred_element_type=jnp.float32)


def kernel(
    nx, ny, nz, heads,
    q_hbm, k_hbm, x_hbm, w_hbm, gc_hbm, len_s, ord_s,
    ctx_o, gq_o, gk_o, gv_o, gw_o,
    q_v, gc_v, x_v, w_v, kv, qn, qt, gcn, gct, bias, kw, vw, kwt, vwt,
    kacc, vacc, pad, sib_out, sib_in, rs_out, rs_in, ctx_v, gq_v, gkv_v,
    xg, xgt, gvg, p_out, p_in, r_v, r_in, gw_v,
    load_sem, store_sem, ring_send, ring_recv, sib_send, sib_recv,
    half_send, half_recv, rs_send, rs_recv, xg_send, xg_recv,
    gv_send, gv_recv, p_send, p_recv, r_send, r_recv,
):
    nc = 2 * nz
    wb = nc // 2 + 1
    pb = nc - wb
    yc = ny // 2
    ng = 2 * nx
    fr = BLOCK // nc
    pairs = heads // 2
    span = wb * BLOCK
    d = lax.axis_index("dp")
    c = lax.axis_index("ctx")
    y = lax.div(d, nx)
    x = lax.rem(d, nx)
    z = lax.div(c, 2)
    k = lax.rem(c, 2)
    g = 2 * x + k
    score_scale = 1.0 / math.sqrt(BLOCK)

    def at_z(other):
        return {"ctx": 2 * lax.rem(other, nz) + k}

    sibling = {"ctx": 2 * z + 1 - k}

    def load(src, dst, n):
        return pltpu.make_async_copy(src, dst, load_sem.at[n])

    load_k = load(k_hbm, kv.at[0, c], 0)
    load_x = load(x_hbm, x_v, 1)
    load_w = load(w_hbm, w_v, 2)
    load_q = load(q_hbm, q_v, 3)
    load_gc = load(gc_hbm, gc_v, 4)
    for one in (load_k, load_x, load_w, load_q, load_gc):
        one.start()

    barrier = pltpu.get_barrier_semaphore()
    count = 0
    for s in range(1, nc):
        pl.semaphore_signal(barrier, 1, device_id={"ctx": lax.rem(c + s, nc)}, device_id_type=MESH)
        count += 1
    for s in range(1, nx):
        for kk in range(2):
            pl.semaphore_signal(
                barrier, 1,
                device_id={"dp": y * nx + lax.rem(x + s, nx), "ctx": 2 * z + kk},
                device_id_type=MESH,
            )
            count += 1
    for s in range(1, ny):
        pl.semaphore_signal(
            barrier, 1, device_id={"dp": lax.rem(y + s, ny) * nx + x}, device_id_type=MESH
        )
        count += 1
    pl.semaphore_wait(barrier, count)

    reach = ((nz // 2, nz - 1 - nz // 2), (nz - 1 - nz // 2, nz // 2))

    def ring(t, zs, way):
        slot = kv.at[t, 2 * zs + k]
        step = 1 if way == 0 else nz - 1
        return remote(slot, slot, ring_send.at[t, way, zs], ring_recv.at[t, zs], at_z(z + step))

    def to_sibling(t, zs):
        slot = kv.at[t, 2 * zs + k]
        return remote(slot, slot, sib_send.at[t, zs], sib_recv.at[t, zs], sibling)

    def origin(way, s):
        return lax.rem(z + nz - s, nz) if way == 0 else lax.rem(z + s, nz)

    def ring_begin(t):
        for way in range(2):
            if reach[t][way] > 0:
                ring(t, z, way).start()
        to_sibling(t, z).start()

    def ring_step(t, s):
        for way in range(2):
            if s <= reach[t][way]:
                zs = origin(way, s)
                ring(t, zs, way).wait_recv()
                if s < reach[t][way]:
                    ring(t, zs, way).start()
                to_sibling(t, zs).start()

    load_k.wait()
    ring_begin(0)

    def x_columns(kk, xx, i):
        return pl.ds(pl.multiple_of(((kk * yc + i) * nx + xx) * BLOCK, BLOCK), BLOCK)

    def group(s):
        gg = lax.rem(g + s, ng)
        xx = lax.div(gg, 2)
        kk = lax.rem(gg, 2)
        return gg, xx, kk, {"dp": y * nx + xx, "ctx": 2 * z + kk}

    for s in range(1, ng):
        gg, xx, kk, device = group(s)
        for i in range(yc):
            remote(
                x_hbm.at[:, x_columns(kk, xx, i)], xg.at[g, i], xg_send.at[gg], xg_recv.at[g], device
            ).start()

    load_x.wait()
    load_w.wait()
    kv[1, c] = dot(x_v[...], w_v[...]).astype(jnp.bfloat16)
    ring_begin(1)

    ring_step(0, 1)

    load_q.wait()
    load_gc.wait()

    def split_heads(src, upright, turned):
        for h in range(heads):
            part = src[:, h * BLOCK : (h + 1) * BLOCK]
            rows = slice((h % 2) * BLOCK, (h % 2 + 1) * BLOCK)
            upright[h // 2, rows, :] = part
            turned[h // 2, :, rows] = part.T

    split_heads(q_v, qn, qt)
    ring_step(1, 1)
    if nz > 2:
        ring_step(0, 2)
    split_heads(gc_v, gcn, gct)
    if nz > 2:
        ring_step(1, 2)

    block = ord_s[0, c]
    first = jnp.maximum(block - (wb - 1), 0)
    query_pos = block * BLOCK + lax.broadcasted_iota(jnp.int32, (1, BLOCK), 1)
    low = jnp.zeros((1, BLOCK), jnp.int32)
    end = jnp.int32(0)
    for i in range(len_s.shape[1]):
        end = end + len_s[0, i]
        low = jnp.where(query_pos >= end, end, low)
    key_pos = first * BLOCK + lax.broadcasted_iota(jnp.int32, (span, BLOCK), 0)
    bias[...] = jnp.where((key_pos >= low) & (key_pos <= query_pos), 0.0, NEG)
    kacc[...] = jnp.zeros_like(kacc)
    vacc[...] = jnp.zeros_like(vacc)
    for t in range(2):
        for i in range(pb + nc):
            if i < pb or i >= pb + wb:
                pad[t, i] = jnp.zeros((BLOCK, BLOCK), jnp.bfloat16)

    for s in range(3, nz // 2 + 1):
        ring_step(0, s)
        ring_step(1, s)
    for t in range(2):
        for zs in range(nz):
            slot = kv.at[t, 2 * zs + 1 - k]
            remote(slot, slot, sib_send.at[t, zs], sib_recv.at[t, zs], sibling).wait_recv()

    for i in range(wb):
        rows = slice(i * BLOCK, (i + 1) * BLOCK)
        key_block = kv[0, first + i]
        value_block = kv[1, first + i]
        kw[rows, :] = key_block
        vw[rows, :] = value_block
        kwt[:, rows] = key_block.T
        vwt[:, rows] = value_block.T
    log_scale = score_scale * math.log2(math.e)

    def attend(p, carry):
        scores = dot(kw[...], qt[p]) + jnp.concatenate([bias[...], bias[...]], axis=1)
        row_max = jnp.max(scores, axis=0, keepdims=True)
        exp_scores = jnp.exp2(scores * log_scale - row_max * log_scale)
        prob = exp_scores * (1.0 / jnp.sum(exp_scores, axis=0, keepdims=True))
        weights = prob.astype(jnp.bfloat16)
        context = dot(vwt[...], weights).astype(jnp.bfloat16)
        turned = gct[p]
        delta = jnp.sum(
            turned.astype(jnp.float32) * context.astype(jnp.float32), axis=0, keepdims=True
        )
        grad_prob = dot(vw[...], turned)
        grad_scores = (prob * (grad_prob - delta)).astype(jnp.bfloat16)
        grad_query = (dot(kwt[...], grad_scores) * score_scale).astype(jnp.bfloat16)
        vacc[...] += dot(weights, gcn[p])
        kacc[...] += dot(grad_scores, qn[p])
        for i in range(2):
            columns = pl.ds(pl.multiple_of((2 * p + i) * BLOCK, BLOCK), BLOCK)
            lanes = slice(i * BLOCK, (i + 1) * BLOCK)
            ctx_v[:, columns] = context[:, lanes].T
            gq_v[:, columns] = grad_query[:, lanes].T
        return carry

    lax.fori_loop(0, pairs, attend, 0)
    store_ctx = pltpu.make_async_copy(ctx_v, ctx_o, store_sem.at[0])
    store_gq = pltpu.make_async_copy(gq_v, gq_o, store_sem.at[1])

    def half(t):
        return remote(sib_out.at[t], sib_in.at[t], half_send.at[t], half_recv.at[t], sibling)

    for t, acc, factor in ((1, vacc, 1.0), (0, kacc, score_scale)):
        for i in range(wb):
            pad[t, pb + i] = (acc[i * BLOCK : (i + 1) * BLOCK, :] * factor).astype(jnp.bfloat16)
        for zs in range(nz):
            sib_out[t, zs] = pad[t, pb + 2 * zs + 1 - k - first]
        half(t).start()
    store_ctx.start()
    store_gq.start()

    def scatter(t, s):
        zs = lax.rem(z + s, nz)
        return remote(
            rs_out.at[t, zs], rs_in.at[t, z], rs_send.at[t, zs], rs_recv.at[t, z], at_z(z + s)
        )

    def pair_sums(t):
        half(t).wait_recv()
        for zs in range(nz):
            both = pad[t, pb + 2 * zs + k - first].astype(jnp.float32) + sib_in[t, zs].astype(
                jnp.float32
            )
            rs_out[t, zs] = both.astype(jnp.bfloat16)

    def gathered(t):
        total = rs_out[t, z].astype(jnp.float32)
        for s in range(1, nz):
            zs = lax.rem(z + s, nz)
            remote(
                rs_out.at[t, zs], rs_in.at[t, zs], rs_send.at[t, zs], rs_recv.at[t, zs], at_z(z + s)
            ).wait_recv()
            total += rs_in[t, zs].astype(jnp.float32)
        return total.astype(jnp.bfloat16)

    pair_sums(1)
    for s in range(1, nz):
        scatter(1, s).start()
    pair_sums(0)

    for s in range(1, ng):
        gg, xx, kk, device = group(s)
        remote(xg.at[gg], xg.at[gg], xg_send.at[gg], xg_recv.at[gg], device).wait_recv()
    for i in range(yc):
        xg[g, i] = x_v[:, x_columns(k, x, i)]
    for gg in range(ng):
        for i in range(yc):
            xgt[i, :, gg * BLOCK : (gg + 1) * BLOCK] = xg[gg, i].T

    grad_values = gathered(1)
    gvg[g] = grad_values

    def share(s):
        gg, xx, kk, device = group(s)
        return remote(gvg.at[g], gvg.at[g], gv_send.at[gg], gv_recv.at[g], device)

    for s in range(1, ng):
        share(s).start()
    for s in range(1, nz):
        scatter(0, s).start()
    store_gv = pltpu.make_async_copy(gvg.at[g], gv_o, store_sem.at[2])
    store_gv.start()
    for s in range(1, ng):
        gg, xx, kk, device = group(s)
        remote(gvg.at[gg], gvg.at[gg], gv_send.at[gg], gv_recv.at[gg], device).wait_recv()

    group_rows = gvg[...].reshape(ng * BLOCK, BLOCK)

    def to_y(i):
        yy = k * yc + i
        return yy, remote(
            p_out.at[i], p_in.at[y], p_send.at[i], p_recv.at[y], {"dp": yy * nx + x}
        )

    for i in range(yc):
        p_out[i] = dot(xgt[i], group_rows).astype(jnp.bfloat16)
        yy, copy = to_y(i)
        pl.when(yy != y)(copy.start)

    collects = lax.div(y, yc) == k

    def to_ctx(s):
        other = lax.rem(c + s, nc)
        rows = pl.ds(pl.multiple_of(other * fr, fr), fr)
        return remote(r_v.at[rows], r_in.at[z], r_send.at[s], r_recv.at[z], {"ctx": other})

    @pl.when(collects)
    def _():
        total = p_out[lax.rem(y, yc)].astype(jnp.float32)
        for s in range(1, ny):
            yy = lax.rem(y + s, ny)
            remote(
                p_in.at[yy], p_in.at[yy], p_send.at[0], p_recv.at[yy], {"dp": yy * nx + x}
            ).wait_recv()
            total += p_in[yy].astype(jnp.float32)
        r_v[...] = total
        for s in range(1, nc):
            to_ctx(s).start()
        r_in[z] = r_v[pl.ds(pl.multiple_of(c * fr, fr), fr), :]

    gkv_v[...] = gathered(0)
    store_gk = pltpu.make_async_copy(gkv_v, gk_o, store_sem.at[3])
    store_gk.start()

    for zs in range(nz):
        @pl.when(jnp.logical_not(collects & (z == zs)))
        def _():
            remote(
                r_in.at[zs], r_in.at[zs], r_send.at[0], r_recv.at[zs], sibling
            ).wait_recv()

    gw_v[...] = jnp.sum(r_in[...], axis=0)
    store_gw = pltpu.make_async_copy(gw_v, gw_o, store_sem.at[4])
    store_gw.start()

    for t in range(2):
        for way in range(2):
            for s in range(reach[t][way]):
                ring(t, origin(way, s), way).wait_send()
        for zs in range(nz):
            to_sibling(t, zs).wait_send()
        half(t).wait_send()
        for s in range(1, nz):
            scatter(t, s).wait_send()
    for s in range(1, ng):
        gg, xx, kk, device = group(s)
        remote(xg.at[gg], xg.at[gg], xg_send.at[gg], xg_recv.at[gg], device).wait_send()
        share(s).wait_send()
    for i in range(yc):
        yy, copy = to_y(i)
        pl.when(yy != y)(copy.wait_send)

    @pl.when(collects)
    def _():
        for s in range(1, nc):
            to_ctx(s).wait_send()

    for one in (store_ctx, store_gq, store_gv, store_gk, store_gw):
        one.wait()


def body(nx, ny, nz, queries, key_rows, x_rows, value_weight, grad_context, doc_lengths, block_order):
    rows, width = queries.shape[1:]
    features = x_rows.shape[2]
    heads = width // BLOCK
    nc = 2 * nz
    wb = nc // 2 + 1
    pb = nc - wb
    yc = ny // 2
    ng = 2 * nx
    fr = BLOCK // nc
    pairs = heads // 2
    span = wb * BLOCK
    bf16, f32 = jnp.bfloat16, jnp.float32
    sq = (BLOCK, BLOCK)
    anywhere = pl.BlockSpec(memory_space=pl.ANY)
    scalars = pl.BlockSpec(memory_space=pltpu.SMEM)
    dma = pltpu.SemaphoreType.DMA
    outs = pl.pallas_call(
        functools.partial(kernel, nx, ny, nz, heads),
        out_shape=(
            jax.ShapeDtypeStruct((rows, width), bf16),
            jax.ShapeDtypeStruct((rows, width), bf16),
            jax.ShapeDtypeStruct(sq, bf16),
            jax.ShapeDtypeStruct(sq, bf16),
            jax.ShapeDtypeStruct((fr, BLOCK), f32),
        ),
        in_specs=[anywhere] * 5 + [scalars] * 2,
        out_specs=(anywhere,) * 5,
        scratch_shapes=[
            pltpu.VMEM((rows, width), bf16),
            pltpu.VMEM((rows, width), bf16),
            pltpu.VMEM((rows, features), bf16),
            pltpu.VMEM((features, BLOCK), bf16),
            pltpu.VMEM((2, nc) + sq, bf16),
            pltpu.VMEM((pairs, 2 * BLOCK, BLOCK), bf16),
            pltpu.VMEM((pairs, BLOCK, 2 * BLOCK), bf16),
            pltpu.VMEM((pairs, 2 * BLOCK, BLOCK), bf16),
            pltpu.VMEM((pairs, BLOCK, 2 * BLOCK), bf16),
            pltpu.VMEM((span, BLOCK), f32),
            pltpu.VMEM((span, BLOCK), bf16),
            pltpu.VMEM((span, BLOCK), bf16),
            pltpu.VMEM((BLOCK, span), bf16),
            pltpu.VMEM((BLOCK, span), bf16),
            pltpu.VMEM((span, BLOCK), f32),
            pltpu.VMEM((span, BLOCK), f32),
            pltpu.VMEM((2, pb + nc) + sq, bf16),
            pltpu.VMEM((2, nz) + sq, bf16),
            pltpu.VMEM((2, nz) + sq, bf16),
            pltpu.VMEM((2, nz) + sq, bf16),
            pltpu.VMEM((2, nz) + sq, bf16),
            pltpu.VMEM((rows, width), bf16),
            pltpu.VMEM((rows, width), bf16),
            pltpu.VMEM(sq, bf16),
            pltpu.VMEM((ng, yc) + sq, bf16),
            pltpu.VMEM((yc, BLOCK, ng * BLOCK), bf16),
            pltpu.VMEM((ng,) + sq, bf16),
            pltpu.VMEM((yc,) + sq, bf16),
            pltpu.VMEM((ny,) + sq, bf16),
            pltpu.VMEM(sq, f32),
            pltpu.VMEM((nz, fr, BLOCK), f32),
            pltpu.VMEM((fr, BLOCK), f32),
            dma((5,)),
            dma((5,)),
            dma((2, 2, nz)),
            dma((2, nz)),
            dma((2, nz)),
            dma((2, nz)),
            dma((2,)),
            dma((2,)),
            dma((2, nz)),
            dma((2, nz)),
            dma((ng,)),
            dma((ng,)),
            dma((ng,)),
            dma((ng,)),
            dma((yc,)),
            dma((ny,)),
            dma((nc,)),
            dma((nz,)),
        ],
        compiler_params=pltpu.CompilerParams(
            collective_id=0, has_side_effects=True, vmem_limit_bytes=40 * 1024 * 1024
        ),
        name="attention_core",
    )(
        queries[0], key_rows[0], x_rows[0], value_weight, grad_context[0], doc_lengths, block_order
    )
    context, grad_queries, grad_keys, grad_values, grad_weight = outs
    return (context[None], grad_queries[None], grad_keys[None], grad_values[None], grad_weight)


def solution(mesh, sizes=(4, 8, 8)):
    placed = (
        P("dp", "ctx", None),
        P("dp", "ctx", None),
        P("dp", "ctx", None),
        P(),
        P("dp", "ctx", None),
        P("dp", None),
        P("dp", None),
    )
    return jax.shard_map(
        functools.partial(body, *sizes),
        mesh=mesh,
        in_specs=placed,
        out_specs=(
            P("dp", "ctx", None),
            P("dp", "ctx", None),
            P("dp", "ctx", None),
            P("dp", "ctx", None),
            P(("dp", "ctx"), None),
        ),
        check_vma=False,
    )
```

time: 435 us -> 76.7 us (0.18)
  waiting for transfers between devices: 378 us -> 0 us
  Pallas kernels: 0 us -> 66.7 us
  matrix products: 14.3 us -> 0 us
  between operations: 13.9 us -> 0.67 us
  other arithmetic: 12.8 us -> 0 us
  local copies, waits for them, and re-layouts: 14.1 us -> 8.99 us
    unnamed x4 -> x0, waiting for transfers between devices: 280 us -> none
    pallas_call x0 -> x1, Pallas kernels: none -> 66.7 us  [body(): pl.pallas_call(functools.partial(kernel, nx, ny, nz, heads), out_shape=(j...]
    reduce_scatter x1 -> x0, waiting for transfers between devices: 56.4 us -> none  [body(): lax.psum_scatter(partial_grads.astype(jnp.bfloat16), 'ctx', scatter_dimen...]
    all_gather x1 -> x0, waiting for transfers between devices: 41.6 us -> none  [body(): all_pairs = lax.all_gather(local_pairs, 'ctx', axis=0, tiled=True)]
    dot_general x14 -> x0, matrix products: 14.3 us -> none  [the longest x1 2.58 us: body(): lax.dot_general(input_local, grad_values, (((0,), (0,)), ((), ())), prefe...]
    reduce_sum x8 -> x0, other arithmetic: 6.2 us -> none  [the longest x2 2.4 us: attend(): prob = exp_scores / jnp.sum(exp_scores, axis=1, keepdims=True)]
    unnamed x15 -> x19, local copies, waits for them, and re-layouts: 3.32 us -> 8.99 us
  transfers between devices with their start and end apart: 3 -> 0, of which waited for: 3 -> 0; matrix products, arithmetic and copies ran while one was open for 2% -> 0% of each run, Pallas kernels for 0% -> 0%
where the time goes in v1:
time: 76.7 us; the launch traced here: 76.4 us
  Pallas kernels  66.7 us (87%)
  local copies, waits for them, and re-layouts  8.99 us (12%)
    pallas_call x1, Pallas kernels, body(): pl.pallas_call(functools.partial(kernel, nx, ny, nz, heads), out_shape=(j...  66.7 us
    unnamed x19, local copies, waits for them, and re-layouts  8.99 us

profile of v1, /device:TPU:1, one launch (start us, length us, event | category | flops | bytes accessed | tf_op | source)
XLA Modules:
  0.0 76.4 jit_solution(9070033825309307000)
XLA Ops:
  0.6 0.0 copy-start.5
  0.6 0.0 copy-start.6
  0.7 0.6 copy-done.5
  1.3 0.0 copy-done.6
  1.3 0.0 copy-start
  1.3 1.2 %copy-done = bf16[1,128,4096]{2,1,0:T(8,128)(2,1)S(1)} copy-done((bf16[1,128,4096]{2,1,0:T(8,128)(2,1)S(1)}, bf16[1,128,4096]{2,1,0:T(8,128)(2,1)}, u32[]{:S(2)}) %copy-start) | copy-done | bytes 1048600
  2.5 0.0 copy-start.1
  2.5 1.2 %copy-done.1 = bf16[4096,128]{1,0:T(8,128)(2,1)S(1)} copy-done((bf16[4096,128]{1,0:T(8,128)(2,1)S(1)}, bf16[4096,128]{1,0:T(8,128)(2,1)}, u32[]{:S(2)}) %copy-start.1) | copy-done | bytes 1048600
  3.8 0.0 copy-start.2
  3.8 0.9 %copy-done.2 = bf16[1,128,1024]{2,1,0:T(8,128)(2,1)S(1)} copy-done((bf16[1,128,1024]{2,1,0:T(8,128)(2,1)S(1)}, bf16[1,128,1024]{2,1,0:T(8,128)(2,1)}, u32[]{:S(2)}) %copy-start.2) | copy-done | bytes 262168
  4.7 0.0 copy-start.3
  4.7 0.9 %copy-done.3 = bf16[1,128,1024]{2,1,0:T(8,128)(2,1)S(1)} copy-done((bf16[1,128,1024]{2,1,0:T(8,128)(2,1)S(1)}, bf16[1,128,1024]{2,1,0:T(8,128)(2,1)}, u32[]{:S(2)}) %copy-start.3) | copy-done | bytes 262168
  5.7 0.0 copy-start.4
  5.7 0.8 copy-done.4
  6.4 66.7 %attention_core.1 = (bf16[128,1024]{1,0:T(8,128)(2,1)S(1)}, bf16[128,1024]{1,0:T(8,128)(2,1)S(1)}, bf16[128,128]{1,0:T(8,128)(2,1)S(1)}, bf16[128,128]{1,0:T(8,128)(2,1)S(1)}, f32[8,128]{1,0:T(8,128)S(1)}) custom-call(bf16[128,1024]{1,0:T(8,128)(2,1)S(1)} %bitcast.9, bf16[128,128]{1,0:T(8,128)(2,1)S(1)} %bitcast.13, bf16[128,4096]{1,0:T(8,128)(2,1)S(1)} %bitcast.8, ...), custom_call_target="tpu_custom_call" | custom-call | tf_op jit(solution)/shard_map/attention_core/pallas_call | solution.py:389
  73.1 0.7 copy.17
  73.8 0.7 copy.18
  74.5 0.6 copy.19
  75.1 0.6 copy.20
  75.8 0.6 copy.21
Async XLA Ops:
  0.6 0.7 copy-start.5
  0.6 0.7 copy-start.6
  1.3 1.2 %copy-start = (bf16[1,128,4096]{2,1,0:T(8,128)(2,1)S(1)}, bf16[1,128,4096]{2,1,0:T(8,128)(2,1)}, u32[]{:S(2)}) copy-start(bf16[1,128,4096]{2,1,0:T(8,128)(2,1)} %param.9) | copy-start | bytes 3145732
  2.5 1.2 %copy-start.1 = (bf16[4096,128]{1,0:T(8,128)(2,1)S(1)}, bf16[4096,128]{1,0:T(8,128)(2,1)}, u32[]{:S(2)}) copy-start(bf16[4096,128]{1,0:T(8,128)(2,1)} %w_hbm.1) | copy-start | bytes 3145732
  3.8 0.9 %copy-start.2 = (bf16[1,128,1024]{2,1,0:T(8,128)(2,1)S(1)}, bf16[1,128,1024]{2,1,0:T(8,128)(2,1)}, u32[]{:S(2)}) copy-start(bf16[1,128,1024]{2,1,0:T(8,128)(2,1)} %param.7) | copy-start | bytes 786436
  4.7 0.9 %copy-start.3 = (bf16[1,128,1024]{2,1,0:T(8,128)(2,1)S(1)}, bf16[1,128,1024]{2,1,0:T(8,128)(2,1)}, u32[]{:S(2)}) copy-start(bf16[1,128,1024]{2,1,0:T(8,128)(2,1)} %param.11) | copy-start | bytes 786436
  5.7 0.8 copy-start.4

commit v2 on v1

v2 whole, which is shorter than its diff:
```python
import functools
import math

import jax
import jax.numpy as jnp
from jax import lax
from jax.experimental import pallas as pl
from jax.experimental.pallas import tpu as pltpu
from jax.sharding import PartitionSpec as P

BLOCK = 128
MESH = pl.DeviceIdType.MESH
NEG = -1e30
VMEM_LIMIT = 60 * 1024 * 1024


def remote(src, dst, send_sem, recv_sem, device):
    return pltpu.make_async_remote_copy(
        src_ref=src,
        dst_ref=dst,
        send_sem=send_sem,
        recv_sem=recv_sem,
        device_id=device,
        device_id_type=MESH,
    )


def dot(a, b):
    return jnp.dot(a, b, preferred_element_type=jnp.float32)


def kernel(
    nx, ny, nz, heads,
    q_hbm, k_hbm, x_hbm, w_hbm, gc_hbm, len_s, ord_s,
    ctx_o, gq_o, gk_o, gv_o, gw_o,
    q_v, gc_v, x_v, w_v, k_all, v_all, qn, qt, gcn, gct, bias, kw, vw, kwt, vwt,
    wt, kacc, vacc, pad, sib_out, sib_in, rs_out, rs_in, ctx_v, gq_v, gkv_v,
    x_out, xg, xgt, gvg, p_out, p_in, r_v, r_in, gw_v,
    load_sem, store_sem, hop_send, hop_recv, far_send, far_recv, sib_send, sib_recv,
    half_send, half_recv, rs_send, rs_recv, xg_send, xg_recv,
    gv_send, gv_recv, p_send, p_recv, r_send, r_recv,
):
    nc = 2 * nz
    wb = nc // 2 + 1
    pb = nc - wb
    yc = ny // 2
    ng = 2 * nx
    fr = BLOCK // nc
    pairs = heads // 2
    span = wb * BLOCK
    d = lax.axis_index("dp")
    c = lax.axis_index("ctx")
    y = lax.div(d, nx)
    x = lax.rem(d, nx)
    z = lax.div(c, 2)
    k = lax.rem(c, 2)
    g = 2 * x + k
    kv = (k_all, v_all)
    score_scale = 1.0 / math.sqrt(BLOCK)

    sibling = {"ctx": 2 * z + 1 - k}

    def load(src, dst, n):
        return pltpu.make_async_copy(src, dst, load_sem.at[n])

    load_k = load(k_hbm, k_all.at[c], 0)
    load_x = load(x_hbm, x_v, 1)
    load_w = load(w_hbm, w_v, 2)
    load_q = load(q_hbm, q_v, 3)
    load_gc = load(gc_hbm, gc_v, 4)
    for one in (load_k, load_x, load_w, load_q, load_gc):
        one.start()

    barrier = pltpu.get_barrier_semaphore()
    partners = [{"ctx": 2 * lax.rem(z + s, nz) + k} for s in range(1, nz)] + [sibling]
    for kk in range(2):
        for s in range(1, nx):
            partners.append({"dp": y * nx + lax.rem(x + s, nx), "ctx": 2 * z + kk})
        for s in range(1, ny):
            partners.append({"dp": lax.rem(y + s, ny) * nx + x, "ctx": 2 * z + kk})
    for device in partners:
        pl.semaphore_signal(barrier, 1, device_id=device, device_id_type=MESH)
    pl.semaphore_wait(barrier, len(partners))

    low_half, high_half = pl.ds(0, BLOCK // 2), pl.ds(BLOCK // 2, BLOCK // 2)

    def at(s):
        return lax.rem(z + (s + 2 * nz), nz)

    def hop(t, zs, s, part=None):
        slot = kv[t].at[2 * zs + k]
        if part is None:
            return remote(
                slot, slot, hop_send.at[t, zs, s + 2], hop_recv.at[t, zs], {"ctx": 2 * at(s) + k}
            )
        slot = slot.at[high_half if part else low_half]
        return remote(
            slot, slot, far_send.at[t, part], far_recv.at[t, part], {"ctx": 2 * at(s) + k}
        )

    def to_sibling(t, zs):
        slot = kv[t].at[2 * zs + k]
        return remote(slot, slot, sib_send.at[t, zs], sib_recv.at[t, zs], sibling)

    near = (2, -2, 1, -1) if nz == 8 else ((1, -1, 2) if nz == 4 else (1,))
    relays = ((-2, 1), (2, -1)) if nz == 8 else ()

    def direct(t):
        for s in near:
            hop(t, z, s).start()
        to_sibling(t, z).start()

    def relay(t):
        for source, s in relays:
            zs = at(source)
            hop(t, zs, s).wait_recv()
            hop(t, zs, 2 * s, 0 if s > 0 else 1).start()
            hop(t, zs, s).start()
            to_sibling(t, zs).start()
        for s in near:
            if s not in (2, -2) or nz != 8:
                hop(t, at(-s), s).wait_recv()
                to_sibling(t, at(-s)).start()

    def settle(t):
        if nz == 8:
            for s in (1, -1):
                zs = at(-3 * s)
                hop(t, zs, s).wait_recv()
                to_sibling(t, zs).start()
            hop(t, at(-4), 2, 0).wait_recv()
            hop(t, at(-4), -2, 1).wait_recv()
            to_sibling(t, at(-4)).start()

    def all_here(t):
        for s in range(nz):
            zs = at(s)
            slot = kv[t].at[2 * zs + 1 - k]
            remote(slot, slot, sib_send.at[t, zs], sib_recv.at[t, zs], sibling).wait_recv()

    load_k.wait()
    direct(0)

    def group(s):
        gg = lax.rem(g + s, ng)
        xx = lax.div(gg, 2)
        kk = lax.rem(gg, 2)
        return gg, xx, kk, {"dp": y * nx + xx, "ctx": 2 * z + kk}

    def columns_to(s):
        gg, xx, kk, device = group(s)
        return remote(x_out.at[gg], xg.at[g], xg_send.at[gg], xg_recv.at[g], device)

    load_x.wait()
    load_w.wait()
    v_all[c] = dot(x_v[...], w_v[...]).astype(jnp.bfloat16)
    for gg in range(ng):
        for i in range(yc):
            column = (((gg % 2) * yc + i) * nx + gg // 2) * BLOCK
            x_out[gg, i] = x_v[:, column : column + BLOCK]
    for s in range(1, ng):
        columns_to(s).start()

    load_q.wait()
    load_gc.wait()
    for h in range(heads):
        part = q_v[:, h * BLOCK : (h + 1) * BLOCK]
        rows = slice((h % 2) * BLOCK, (h % 2 + 1) * BLOCK)
        qn[h // 2, rows, :] = part
        qt[h // 2, :, rows] = part.T
        gcn[h // 2, rows, :] = gc_v[:, h * BLOCK : (h + 1) * BLOCK]

    relay(0)
    direct(1)

    block = ord_s[0, c]
    first = jnp.maximum(block - (wb - 1), 0)
    query_pos = block * BLOCK + lax.broadcasted_iota(jnp.int32, (1, BLOCK), 1)
    low = jnp.zeros((1, BLOCK), jnp.int32)
    end = jnp.int32(0)
    for i in range(len_s.shape[1]):
        end = end + len_s[0, i]
        low = jnp.where(query_pos >= end, end, low)
    key_pos = first * BLOCK + lax.broadcasted_iota(jnp.int32, (span, BLOCK), 0)
    bias[...] = jnp.where((key_pos >= low) & (key_pos <= query_pos), 0.0, NEG)
    kacc[...] = jnp.zeros_like(kacc)
    vacc[...] = jnp.zeros_like(vacc)
    for t in range(2):
        for i in range(pb + nc):
            if i < pb or i >= pb + wb:
                pad[t, i] = jnp.zeros((BLOCK, BLOCK), jnp.bfloat16)
    for h in range(heads):
        rows = slice((h % 2) * BLOCK, (h % 2 + 1) * BLOCK)
        gct[h // 2, :, rows] = gc_v[:, h * BLOCK : (h + 1) * BLOCK].T

    settle(0)
    all_here(0)

    for i in range(wb):
        kw[i * BLOCK : (i + 1) * BLOCK, :] = k_all[first + i]
    log_scale = score_scale * math.log2(math.e)

    def weigh(p, carry):
        scores = dot(kw[...], qt[p]) + jnp.concatenate([bias[...], bias[...]], axis=1)
        row_max = jnp.max(scores, axis=0, keepdims=True)
        exp_scores = jnp.exp2(scores * log_scale - row_max * log_scale)
        weights = (exp_scores * (1.0 / jnp.sum(exp_scores, axis=0, keepdims=True))).astype(
            jnp.bfloat16
        )
        wt[p] = weights
        vacc[...] += dot(weights, gcn[p])
        return carry

    lax.fori_loop(0, pairs // 2, weigh, 0)
    relay(1)
    lax.fori_loop(pairs // 2, pairs, weigh, 0)

    def half(t):
        return remote(sib_out.at[t], sib_in.at[t], half_send.at[t], half_recv.at[t], sibling)

    def swap_halves(t, acc, factor):
        for i in range(wb):
            pad[t, pb + i] = (acc[i * BLOCK : (i + 1) * BLOCK, :] * factor).astype(jnp.bfloat16)
        for zs in range(nz):
            sib_out[t, zs] = pad[t, pb + 2 * zs + 1 - k - first]
        half(t).start()

    def scatter(t, s):
        return remote(
            rs_out.at[t, at(s)], rs_in.at[t, z], rs_send.at[t, at(s)], rs_recv.at[t, z],
            {"ctx": 2 * at(s) + k},
        )

    def scatter_sums(t):
        half(t).wait_recv()
        for zs in range(nz):
            both = pad[t, pb + 2 * zs + k - first].astype(jnp.float32) + sib_in[t, zs].astype(
                jnp.float32
            )
            rs_out[t, zs] = both.astype(jnp.bfloat16)
        for s in sorted(range(1, nz), key=lambda s: -min(s, nz - s)):
            scatter(t, s).start()

    def gathered(t):
        total = rs_out[t, z].astype(jnp.float32)
        for s in sorted(range(1, nz), key=lambda s: min(s, nz - s)):
            zs = at(s)
            remote(
                rs_out.at[t, zs], rs_in.at[t, zs], rs_send.at[t, zs], rs_recv.at[t, zs],
                {"ctx": 2 * zs + k},
            ).wait_recv()
            total += rs_in[t, zs].astype(jnp.float32)
        return total.astype(jnp.bfloat16)

    swap_halves(1, vacc, 1.0)
    settle(1)
    scatter_sums(1)

    for i in range(wb):
        kwt[:, i * BLOCK : (i + 1) * BLOCK] = kw[i * BLOCK : (i + 1) * BLOCK, :].T
    all_here(1)
    for i in range(wb):
        value_block = v_all[first + i]
        vw[i * BLOCK : (i + 1) * BLOCK, :] = value_block
        vwt[:, i * BLOCK : (i + 1) * BLOCK] = value_block.T

    def attend(p, carry):
        weights = wt[p]
        turned = gct[p]
        context = dot(vwt[...], weights).astype(jnp.bfloat16)
        delta = jnp.sum(
            turned.astype(jnp.float32) * context.astype(jnp.float32), axis=0, keepdims=True
        )
        grad_prob = dot(vw[...], turned)
        grad_scores = (weights.astype(jnp.float32) * (grad_prob - delta)).astype(jnp.bfloat16)
        grad_query = (dot(kwt[...], grad_scores) * score_scale).astype(jnp.bfloat16)
        kacc[...] += dot(grad_scores, qn[p])
        for i in range(2):
            columns = pl.ds(pl.multiple_of((2 * p + i) * BLOCK, BLOCK), BLOCK)
            lanes = slice(i * BLOCK, (i + 1) * BLOCK)
            ctx_v[:, columns] = context[:, lanes].T
            gq_v[:, columns] = grad_query[:, lanes].T
        return carry

    lax.fori_loop(0, pairs, attend, 0)
    store_ctx = pltpu.make_async_copy(ctx_v, ctx_o, store_sem.at[0])
    store_gq = pltpu.make_async_copy(gq_v, gq_o, store_sem.at[1])
    swap_halves(0, kacc, score_scale)
    store_ctx.start()
    store_gq.start()

    for s in range(1, ng):
        gg, xx, kk, device = group(s)
        remote(xg.at[gg], xg.at[gg], xg_send.at[gg], xg_recv.at[gg], device).wait_recv()
    xg[g] = x_out[g]
    for gg in range(ng):
        for i in range(yc):
            xgt[i, :, gg * BLOCK : (gg + 1) * BLOCK] = xg[gg, i].T

    gvg[g] = gathered(1)

    def share(s):
        gg, xx, kk, device = group(s)
        return remote(gvg.at[g], gvg.at[g], gv_send.at[gg], gv_recv.at[g], device)

    for s in range(1, ng):
        share(s).start()
    scatter_sums(0)
    store_gv = pltpu.make_async_copy(gvg.at[g], gv_o, store_sem.at[2])
    store_gv.start()
    for s in range(1, ng):
        gg, xx, kk, device = group(s)
        remote(gvg.at[gg], gvg.at[gg], gv_send.at[gg], gv_recv.at[gg], device).wait_recv()

    group_rows = gvg[...].reshape(ng * BLOCK, BLOCK)
    source_core = lax.div(y, yc)

    def to_y(i, kk):
        yy = k * yc + i
        return (yy != y) | (kk != k), remote(
            p_out.at[i, kk], p_in.at[y], p_send.at[i, kk], p_recv.at[y],
            {"dp": yy * nx + x, "ctx": 2 * z + kk},
        )

    for i in range(yc):
        product = dot(xgt[i], group_rows).reshape(nz, 2, fr, BLOCK)
        for kk in range(2):
            p_out[i, kk] = product[:, kk].reshape(nz * fr, BLOCK).astype(jnp.bfloat16)
            away, copy = to_y(i, kk)
            pl.when(away)(copy.start)

    @pl.when(source_core == k)
    def _():
        p_in[y] = p_out[lax.rem(y, yc), k]

    total = jnp.zeros((nz * fr, BLOCK), jnp.float32)
    for s in range(ny):
        yy = lax.rem(y + s, ny)
        copy = remote(
            p_in.at[yy], p_in.at[yy], p_send.at[0, 0], p_recv.at[yy],
            {"dp": yy * nx + x, "ctx": 2 * z + 1 - k},
        )
        if s == 0:
            pl.when(source_core != k)(copy.wait_recv)
        else:
            copy.wait_recv()
        total += p_in[yy].astype(jnp.float32)
    r_v[...] = total

    def to_z(s):
        zs = at(s)
        rows = pl.ds(pl.multiple_of(zs * fr, fr), fr)
        return remote(
            r_v.at[rows], r_in.at[z], r_send.at[zs], r_recv.at[z], {"ctx": 2 * zs + k}
        )

    for s in sorted(range(1, nz), key=lambda s: -min(s, nz - s)):
        to_z(s).start()

    gkv_v[...] = gathered(0)
    store_gk = pltpu.make_async_copy(gkv_v, gk_o, store_sem.at[3])
    store_gk.start()

    total = r_v[pl.ds(pl.multiple_of(z * fr, fr), fr), :]
    for s in sorted(range(1, nz), key=lambda s: min(s, nz - s)):
        zs = at(s)
        remote(
            r_in.at[zs], r_in.at[zs], r_send.at[zs], r_recv.at[zs], {"ctx": 2 * zs + k}
        ).wait_recv()
        total += r_in[zs]
    gw_v[...] = total
    store_gw = pltpu.make_async_copy(gw_v, gw_o, store_sem.at[4])
    store_gw.start()

    for t in range(2):
        for s in near:
            hop(t, z, s).wait_send()
        for source, s in relays:
            hop(t, at(source), 2 * s, 0 if s > 0 else 1).wait_send()
            hop(t, at(source), s).wait_send()
        for zs in range(nz):
            to_sibling(t, zs).wait_send()
        half(t).wait_send()
        for s in range(1, nz):
            scatter(t, s).wait_send()
    for s in range(1, ng):
        columns_to(s).wait_send()
        share(s).wait_send()
    for i in range(yc):
        for kk in range(2):
            away, copy = to_y(i, kk)
            pl.when(away)(copy.wait_send)
    for s in range(1, nz):
        to_z(s).wait_send()

    for one in (store_ctx, store_gq, store_gv, store_gk, store_gw):
        one.wait()


def write_out(*refs):
    held, sems = refs[10:15], refs[15]
    for i in range(5):
        pltpu.make_async_copy(refs[i], held[i], sems.at[0, i]).start()
    for i in range(5):
        pltpu.make_async_copy(refs[i], held[i], sems.at[0, i]).wait()
        pltpu.make_async_copy(held[i], refs[5 + i], sems.at[1, i]).start()
    for i in range(5):
        pltpu.make_async_copy(held[i], refs[5 + i], sems.at[1, i]).wait()


def body(nx, ny, nz, queries, key_rows, x_rows, value_weight, grad_context, doc_lengths, block_order):
    rows, width = queries.shape[1:]
    features = x_rows.shape[2]
    heads = width // BLOCK
    nc = 2 * nz
    wb = nc // 2 + 1
    pb = nc - wb
    yc = ny // 2
    ng = 2 * nx
    fr = BLOCK // nc
    pairs = heads // 2
    span = wb * BLOCK
    bf16, f32 = jnp.bfloat16, jnp.float32
    sq = (BLOCK, BLOCK)
    anywhere = pl.BlockSpec(memory_space=pltpu.HBM)
    scalars = pl.BlockSpec(memory_space=pltpu.SMEM)
    dma = pltpu.SemaphoreType.DMA
    outs = pl.pallas_call(
        functools.partial(kernel, nx, ny, nz, heads),
        out_shape=(
            jax.ShapeDtypeStruct((rows, width), bf16),
            jax.ShapeDtypeStruct((rows, width), bf16),
            jax.ShapeDtypeStruct(sq, bf16),
            jax.ShapeDtypeStruct(sq, bf16),
            jax.ShapeDtypeStruct((fr, BLOCK), f32),
        ),
        in_specs=[anywhere] * 5 + [scalars] * 2,
        out_specs=(anywhere,) * 5,
        scratch_shapes=[
            pltpu.VMEM((rows, width), bf16),
            pltpu.VMEM((rows, width), bf16),
            pltpu.VMEM((rows, features), bf16),
            pltpu.VMEM((features, BLOCK), bf16),
            pltpu.VMEM((nc,) + sq, bf16),
            pltpu.VMEM((nc,) + sq, bf16),
            pltpu.VMEM((pairs, 2 * BLOCK, BLOCK), bf16),
            pltpu.VMEM((pairs, BLOCK, 2 * BLOCK), bf16),
            pltpu.VMEM((pairs, 2 * BLOCK, BLOCK), bf16),
            pltpu.VMEM((pairs, BLOCK, 2 * BLOCK), bf16),
            pltpu.VMEM((span, BLOCK), f32),
            pltpu.VMEM((span, BLOCK), bf16),
            pltpu.VMEM((span, BLOCK), bf16),
            pltpu.VMEM((BLOCK, span), bf16),
            pltpu.VMEM((BLOCK, span), bf16),
            pltpu.VMEM((pairs, span, 2 * BLOCK), bf16),
            pltpu.VMEM((span, BLOCK), f32),
            pltpu.VMEM((span, BLOCK), f32),
            pltpu.VMEM((2, pb + nc) + sq, bf16),
            pltpu.VMEM((2, nz) + sq, bf16),
            pltpu.VMEM((2, nz) + sq, bf16),
            pltpu.VMEM((2, nz) + sq, bf16),
            pltpu.VMEM((2, nz) + sq, bf16),
            pltpu.VMEM((rows, width), bf16),
            pltpu.VMEM((rows, width), bf16),
            pltpu.VMEM(sq, bf16),
            pltpu.VMEM((ng, yc) + sq, bf16),
            pltpu.VMEM((ng, yc) + sq, bf16),
            pltpu.VMEM((yc, BLOCK, ng * BLOCK), bf16),
            pltpu.VMEM((ng,) + sq, bf16),
            pltpu.VMEM((yc, 2, nz * fr, BLOCK), bf16),
            pltpu.VMEM((ny, nz * fr, BLOCK), bf16),
            pltpu.VMEM((nz * fr, BLOCK), f32),
            pltpu.VMEM((nz, fr, BLOCK), f32),
            pltpu.VMEM((fr, BLOCK), f32),
            dma((5,)),
            dma((5,)),
            dma((2, nz, 5)),
            dma((2, nz)),
            dma((2, 2)),
            dma((2, 2)),
            dma((2, nz)),
            dma((2, nz)),
            dma((2,)),
            dma((2,)),
            dma((2, nz)),
            dma((2, nz)),
            dma((ng,)),
            dma((ng,)),
            dma((ng,)),
            dma((ng,)),
            dma((yc, 2)),
            dma((ny,)),
            dma((nz,)),
            dma((nz,)),
        ],
        compiler_params=pltpu.CompilerParams(
            collective_id=0, has_side_effects=True, vmem_limit_bytes=VMEM_LIMIT
        ),
        name="attention_core",
    )(
        queries[0], key_rows[0], x_rows[0], value_weight, grad_context[0], doc_lengths, block_order
    )
    context, grad_queries, grad_keys, grad_values, grad_weight = pl.pallas_call(
        write_out,
        out_shape=tuple(jax.ShapeDtypeStruct(one.shape, one.dtype) for one in outs),
        in_specs=[anywhere] * 5,
        out_specs=(anywhere,) * 5,
        scratch_shapes=[pltpu.VMEM(one.shape, one.dtype) for one in outs] + [dma((2, 5))],
        compiler_params=pltpu.CompilerParams(vmem_limit_bytes=VMEM_LIMIT),
        name="write_out",
    )(*outs)
    return (context[None], grad_queries[None], grad_keys[None], grad_values[None], grad_weight)


def solution(mesh, sizes=(4, 8, 8)):
    placed = (
        P("dp", "ctx", None),
        P("dp", "ctx", None),
        P("dp", "ctx", None),
        P(),
        P("dp", "ctx", None),
        P("dp", None),
        P("dp", None),
    )
    return jax.shard_map(
        functools.partial(body, *sizes),
        mesh=mesh,
        in_specs=placed,
        out_specs=(
            P("dp", "ctx", None),
            P("dp", "ctx", None),
            P("dp", "ctx", None),
            P("dp", "ctx", None),
            P(("dp", "ctx"), None),
        ),
        check_vma=False,
    )
```

time: 76.7 us -> 59.9 us (0.78)
  local copies, waits for them, and re-layouts: 8.99 us -> 0 us
  Pallas kernels: 66.7 us -> 59.1 us
    pallas_call x1, Pallas kernels: 66.7 us -> 57.3 us  [body(): pl.pallas_call(functools.partial(kernel, nx, ny, nz, heads), out_shape=(j...]
    unnamed x19 -> x0, local copies, waits for them, and re-layouts: 8.99 us -> none
    pallas_call x0 -> x1, Pallas kernels: none -> 1.84 us  [body(): pl.pallas_call(write_out, out_shape=tuple((jax.ShapeDtypeStruct(one.shape...]
where the time goes in v2:
time: 59.9 us; the launch traced here: 59.8 us
  Pallas kernels  59.1 us (99%)
  between operations  0.64 us (1%)
    pallas_call x1, Pallas kernels, body(): pl.pallas_call(functools.partial(kernel, nx, ny, nz, heads), out_shape=(j...  57.3 us
    pallas_call x1, Pallas kernels, body(): pl.pallas_call(write_out, out_shape=tuple((jax.ShapeDtypeStruct(one.shape...  1.84 us

profile of v2, /device:TPU:1, one launch (start us, length us, event | category | flops | bytes accessed | tf_op | source)
XLA Modules:
  0.0 59.8 jit_solution(17581045934382544253)
XLA Ops:
  0.6 57.3 %attention_core.1 = (bf16[128,1024]{1,0:T(8,128)(2,1)}, bf16[128,1024]{1,0:T(8,128)(2,1)}, bf16[128,128]{1,0:T(8,128)(2,1)}, bf16[128,128]{1,0:T(8,128)(2,1)}, f32[8,128]{1,0:T(8,128)}) custom-call(bf16[128,1024]{1,0:T(8,128)(2,1)} %bitcast.9, bf16[128,128]{1,0:T(8,128)(2,1)} %bitcast.11, bf16[128,4096]{1,0:T(8,128)(2,1)} %bitcast.8, ...), custom_call_target="tpu_custom_call" | custom-call | tf_op jit(solution)/shard_map/attention_core/pallas_call | solution.py:428
  57.9 1.8 %write_out.1 = (bf16[128,1024]{1,0:T(8,128)(2,1)}, bf16[128,1024]{1,0:T(8,128)(2,1)}, bf16[128,128]{1,0:T(8,128)(2,1)}, bf16[128,128]{1,0:T(8,128)(2,1)}, f32[8,128]{1,0:T(8,128)}) custom-call(bf16[128,1024]{1,0:T(8,128)(2,1)} %get-tuple-element.15.refs_0_, bf16[128,1024]{1,0:T(8,128)(2,1)} %get-tuple-element.16.refs_1_, ...), custom_call_target="tpu_custom_call" | custom-call | tf_op jit(solution)/shard_map/write_out/pallas_call | solution.py:503

commit v3 on v2

--- a/solution.py
+++ b/solution.py
@@ -36,7 +36,7 @@
     q_v, gc_v, x_v, w_v, k_all, v_all, qn, qt, gcn, gct, bias, kw, vw, kwt, vwt,
     wt, kacc, vacc, pad, sib_out, sib_in, rs_out, rs_in, ctx_v, gq_v, gkv_v,
     x_out, xg, xgt, gvg, p_out, p_in, r_v, r_in, gw_v,
-    load_sem, store_sem, hop_send, hop_recv, far_send, far_recv, sib_send, sib_recv,
+    ready, load_sem, store_sem, hop_send, hop_recv, sib_send, sib_recv,
     half_send, half_recv, rs_send, rs_recv, xg_send, xg_recv,
     gv_send, gv_recv, p_send, p_recv, r_send, r_recv,
 ):
@@ -72,74 +72,81 @@
         one.start()
 
     barrier = pltpu.get_barrier_semaphore()
-    partners = [{"ctx": 2 * lax.rem(z + s, nz) + k} for s in range(1, nz)] + [sibling]
-    for kk in range(2):
-        for s in range(1, nx):
-            partners.append({"dp": y * nx + lax.rem(x + s, nx), "ctx": 2 * z + kk})
-        for s in range(1, ny):
-            partners.append({"dp": lax.rem(y + s, ny) * nx + x, "ctx": 2 * z + kk})
+
+    def around(n, most):
+        return sorted({s % n for s in range(-most, most + 1)} - {0})
+
+    planar = [{"dp": y * nx + lax.rem(x + s, nx)} for s in around(nx, 1)]
+    planar += [{"dp": lax.rem(y + s, ny) * nx + x} for s in around(ny, 1)]
+    planar.append(sibling)
+    partners = planar + [{"ctx": 2 * lax.rem(z + s, nz) + k} for s in around(nz, 2)]
     for device in partners:
         pl.semaphore_signal(barrier, 1, device_id=device, device_id_type=MESH)
     pl.semaphore_wait(barrier, len(partners))
 
-    low_half, high_half = pl.ds(0, BLOCK // 2), pl.ds(BLOCK // 2, BLOCK // 2)
+    def tell(n):
+        for device in planar:
+            pl.semaphore_signal(ready.at[n], 1, device_id=device, device_id_type=MESH)
+
+    def hear(n):
+        pl.semaphore_wait(ready.at[n], len(planar))
+
 
     def at(s):
         return lax.rem(z + (s + 2 * nz), nz)
 
-    def hop(t, zs, s, part=None):
+    def hop(t, zs, s, kind, part=None):
         slot = kv[t].at[2 * zs + k]
-        if part is None:
-            return remote(
-                slot, slot, hop_send.at[t, zs, s + 2], hop_recv.at[t, zs], {"ctx": 2 * at(s) + k}
-            )
-        slot = slot.at[high_half if part else low_half]
-        return remote(
-            slot, slot, far_send.at[t, part], far_recv.at[t, part], {"ctx": 2 * at(s) + k}
-        )
+        if part is not None:
+            slot = slot.at[pl.ds(part * (BLOCK // 2), BLOCK // 2)]
+        return remote(slot, slot, hop_send.at[t], hop_recv.at[t, kind], {"ctx": 2 * at(s) + k})
+
+    def hops(t, kind, count):
+        slots = kv[t].at[pl.ds(0, count)]
+        return remote(slots, slots, hop_send.at[t], hop_recv.at[t, kind], sibling)
 
     def to_sibling(t, zs):
         slot = kv[t].at[2 * zs + k]
-        return remote(slot, slot, sib_send.at[t, zs], sib_recv.at[t, zs], sibling)
-
-    near = (2, -2, 1, -1) if nz == 8 else ((1, -1, 2) if nz == 4 else (1,))
-    relays = ((-2, 1), (2, -1)) if nz == 8 else ()
+        return remote(slot, slot, sib_send.at[t], sib_recv.at[t], sibling)
+
+    def all_siblings(t):
+        slots = kv[t].at[pl.ds(0, nz)]
+        return remote(slots, slots, sib_send.at[t], sib_recv.at[t], sibling)
+
+    relayed = nz == 8
+    close = (1, -1) if nz > 2 else (1,)
+    if nz == 4:
+        close = (2, 1, -1)
 
     def direct(t):
-        for s in near:
-            hop(t, z, s).start()
+        if relayed:
+            hop(t, z, 2, 0).start()
+            hop(t, z, -2, 1).start()
+        for s in close:
+            hop(t, z, s, 2).start()
         to_sibling(t, z).start()
 
     def relay(t):
-        for source, s in relays:
-            zs = at(source)
-            hop(t, zs, s).wait_recv()
-            hop(t, zs, 2 * s, 0 if s > 0 else 1).start()
-            hop(t, zs, s).start()
-            to_sibling(t, zs).start()
-        for s in near:
-            if s not in (2, -2) or nz != 8:
-                hop(t, at(-s), s).wait_recv()
-                to_sibling(t, at(-s)).start()
+        if relayed:
+            for kind, s in ((0, 1), (1, -1)):
+                zs = at(-2 * s)
+                hops(t, kind, 1).wait_recv()
+                hop(t, zs, 2 * s, 3, kind).start()
+                hop(t, zs, s, 3).start()
+                to_sibling(t, zs).start()
+        hops(t, 2, len(close)).wait_recv()
+        for s in close:
+            to_sibling(t, at(-s)).start()
 
     def settle(t):
-        if nz == 8:
-            for s in (1, -1):
-                zs = at(-3 * s)
-                hop(t, zs, s).wait_recv()
-                to_sibling(t, zs).start()
-            hop(t, at(-4), 2, 0).wait_recv()
-            hop(t, at(-4), -2, 1).wait_recv()
-            to_sibling(t, at(-4)).start()
-
-    def all_here(t):
-        for s in range(nz):
-            zs = at(s)
-            slot = kv[t].at[2 * zs + 1 - k]
-            remote(slot, slot, sib_send.at[t, zs], sib_recv.at[t, zs], sibling).wait_recv()
+        if relayed:
+            hops(t, 3, 3).wait_recv()
+            for s in (3, -3, 4):
+                to_sibling(t, at(s)).start()
 
     load_k.wait()
     direct(0)
+    tell(0)
 
     def group(s):
         gg = lax.rem(g + s, ng)
@@ -149,7 +156,10 @@
 
     def columns_to(s):
         gg, xx, kk, device = group(s)
-        return remote(x_out.at[gg], xg.at[g], xg_send.at[gg], xg_recv.at[g], device)
+        return remote(x_out.at[gg], xg.at[g], xg_send, xg_recv, device)
+
+    def all_columns():
+        return remote(x_out.at[pl.ds(0, ng - 1)], xg.at[pl.ds(0, ng - 1)], xg_send, xg_recv, sibling)
 
     load_x.wait()
     load_w.wait()
@@ -158,9 +168,6 @@
         for i in range(yc):
             column = (((gg % 2) * yc + i) * nx + gg // 2) * BLOCK
             x_out[gg, i] = x_v[:, column : column + BLOCK]
-    for s in range(1, ng):
-        columns_to(s).start()
-
     load_q.wait()
     load_gc.wait()
     for h in range(heads):
@@ -172,6 +179,8 @@
 
     relay(0)
     direct(1)
+    hear(0)
+    tell(1)
 
     block = ord_s[0, c]
     first = jnp.maximum(block - (wb - 1), 0)
@@ -194,7 +203,11 @@
         gct[h // 2, :, rows] = gc_v[:, h * BLOCK : (h + 1) * BLOCK].T
 
     settle(0)
-    all_here(0)
+    hear(1)
+    tell(2)
+    for s in range(1, ng):
+        columns_to(s).start()
+    all_siblings(0).wait_recv()
 
     for i in range(wb):
         kw[i * BLOCK : (i + 1) * BLOCK, :] = k_all[first + i]
@@ -211,9 +224,9 @@
         vacc[...] += dot(weights, gcn[p])
         return carry
 
-    lax.fori_loop(0, pairs // 2, weigh, 0)
+    lax.fori_loop(0, pairs // 2, weigh, 0, unroll=True)
     relay(1)
-    lax.fori_loop(pairs // 2, pairs, weigh, 0)
+    lax.fori_loop(pairs // 2, pairs, weigh, 0, unroll=True)
 
     def half(t):
         return remote(sib_out.at[t], sib_in.at[t], half_send.at[t], half_recv.at[t], sibling)
@@ -227,8 +240,14 @@
 
     def scatter(t, s):
         return remote(
-            rs_out.at[t, at(s)], rs_in.at[t, z], rs_send.at[t, at(s)], rs_recv.at[t, z],
+            rs_out.at[t, at(s)], rs_in.at[t, z], rs_send.at[t], rs_recv.at[t],
             {"ctx": 2 * at(s) + k},
+        )
+
+    def all_scattered(t):
+        return remote(
+            rs_out.at[t, pl.ds(0, nz - 1)], rs_in.at[t, pl.ds(0, nz - 1)],
+            rs_send.at[t], rs_recv.at[t], sibling,
         )
 
     def scatter_sums(t):
@@ -242,23 +261,21 @@
             scatter(t, s).start()
 
     def gathered(t):
+        all_scattered(t).wait_recv()
         total = rs_out[t, z].astype(jnp.float32)
-        for s in sorted(range(1, nz), key=lambda s: min(s, nz - s)):
-            zs = at(s)
-            remote(
-                rs_out.at[t, zs], rs_in.at[t, zs], rs_send.at[t, zs], rs_recv.at[t, zs],
-                {"ctx": 2 * zs + k},
-            ).wait_recv()
-            total += rs_in[t, zs].astype(jnp.float32)
+        for s in range(1, nz):
+            total += rs_in[t, at(s)].astype(jnp.float32)
         return total.astype(jnp.bfloat16)
 
     swap_halves(1, vacc, 1.0)
     settle(1)
     scatter_sums(1)
+    hear(2)
+    tell(3)
 
     for i in range(wb):
         kwt[:, i * BLOCK : (i + 1) * BLOCK] = kw[i * BLOCK : (i + 1) * BLOCK, :].T
-    all_here(1)
+    all_siblings(1).wait_recv()
     for i in range(wb):
         value_block = v_all[first + i]
         vw[i * BLOCK : (i + 1) * BLOCK, :] = value_block
@@ -282,35 +299,36 @@
             gq_v[:, columns] = grad_query[:, lanes].T
         return carry
 
-    lax.fori_loop(0, pairs, attend, 0)
+    lax.fori_loop(0, pairs, attend, 0, unroll=True)
     store_ctx = pltpu.make_async_copy(ctx_v, ctx_o, store_sem.at[0])
     store_gq = pltpu.make_async_copy(gq_v, gq_o, store_sem.at[1])
     swap_halves(0, kacc, score_scale)
     store_ctx.start()
     store_gq.start()
 
+    gvg[g] = gathered(1)
+
+    def share(s):
+        gg, xx, kk, device = group(s)
+        return remote(gvg.at[g], gvg.at[g], gv_send, gv_recv, device)
+
+    def all_shared():
+        return remote(gvg.at[pl.ds(0, ng - 1)], gvg.at[pl.ds(0, ng - 1)], gv_send, gv_recv, sibling)
+
     for s in range(1, ng):
-        gg, xx, kk, device = group(s)
-        remote(xg.at[gg], xg.at[gg], xg_send.at[gg], xg_recv.at[gg], device).wait_recv()
+        share(s).start()
+    scatter_sums(0)
+
+    all_columns().wait_recv()
     xg[g] = x_out[g]
     for gg in range(ng):
         for i in range(yc):
             xgt[i, :, gg * BLOCK : (gg + 1) * BLOCK] = xg[gg, i].T
-
-    gvg[g] = gathered(1)
-
-    def share(s):
-        gg, xx, kk, device = group(s)
-        return remote(gvg.at[g], gvg.at[g], gv_send.at[gg], gv_recv.at[g], device)
-
-    for s in range(1, ng):
-        share(s).start()
-    scatter_sums(0)
+    hear(3)
+
     store_gv = pltpu.make_async_copy(gvg.at[g], gv_o, store_sem.at[2])
     store_gv.start()
-    for s in range(1, ng):
-        gg, xx, kk, device = group(s)
-        remote(gvg.at[gg], gvg.at[gg], gv_send.at[gg], gv_recv.at[gg], device).wait_recv()
+    all_shared().wait_recv()
 
     group_rows = gvg[...].reshape(ng * BLOCK, BLOCK)
     source_core = lax.div(y, yc)
@@ -318,40 +336,36 @@
     def to_y(i, kk):
         yy = k * yc + i
         return (yy != y) | (kk != k), remote(
-            p_out.at[i, kk], p_in.at[y], p_send.at[i, kk], p_recv.at[y],
+            p_out.at[2 * i + kk], p_in.at[y], p_send, p_recv,
             {"dp": yy * nx + x, "ctx": 2 * z + kk},
         )
+
+    def all_y(count):
+        return remote(p_out.at[pl.ds(0, count)], p_in.at[pl.ds(0, count)], p_send, p_recv, sibling)
 
     for i in range(yc):
         product = dot(xgt[i], group_rows).reshape(nz, 2, fr, BLOCK)
         for kk in range(2):
-            p_out[i, kk] = product[:, kk].reshape(nz * fr, BLOCK).astype(jnp.bfloat16)
+            p_out[2 * i + kk] = product[:, kk].reshape(nz * fr, BLOCK).astype(jnp.bfloat16)
             away, copy = to_y(i, kk)
             pl.when(away)(copy.start)
 
     @pl.when(source_core == k)
     def _():
-        p_in[y] = p_out[lax.rem(y, yc), k]
-
-    total = jnp.zeros((nz * fr, BLOCK), jnp.float32)
-    for s in range(ny):
-        yy = lax.rem(y + s, ny)
-        copy = remote(
-            p_in.at[yy], p_in.at[yy], p_send.at[0, 0], p_recv.at[yy],
-            {"dp": yy * nx + x, "ctx": 2 * z + 1 - k},
-        )
-        if s == 0:
-            pl.when(source_core != k)(copy.wait_recv)
-        else:
-            copy.wait_recv()
-        total += p_in[yy].astype(jnp.float32)
-    r_v[...] = total
+        all_y(ny - 1).wait_recv()
+        p_in[y] = p_out[2 * lax.rem(y, yc) + k]
+
+    @pl.when(source_core != k)
+    def _():
+        all_y(ny).wait_recv()
+
+    r_v[...] = jnp.sum(p_in[...].astype(jnp.float32), axis=0)
 
     def to_z(s):
         zs = at(s)
         rows = pl.ds(pl.multiple_of(zs * fr, fr), fr)
         return remote(
-            r_v.at[rows], r_in.at[z], r_send.at[zs], r_recv.at[z], {"ctx": 2 * zs + k}
+            r_v.at[rows], r_in.at[z], r_send, r_recv, {"ctx": 2 * zs + k}
         )
 
     for s in sorted(range(1, nz), key=lambda s: -min(s, nz - s)):
@@ -361,37 +375,29 @@
     store_gk = pltpu.make_async_copy(gkv_v, gk_o, store_sem.at[3])
     store_gk.start()
 
+    def all_z():
+        return remote(
+            r_in.at[pl.ds(0, nz - 1)], r_in.at[pl.ds(0, nz - 1)], r_send, r_recv, sibling
+        )
+
+    all_z().wait_recv()
     total = r_v[pl.ds(pl.multiple_of(z * fr, fr), fr), :]
-    for s in sorted(range(1, nz), key=lambda s: min(s, nz - s)):
-        zs = at(s)
-        remote(
-            r_in.at[zs], r_in.at[zs], r_send.at[zs], r_recv.at[zs], {"ctx": 2 * zs + k}
-        ).wait_recv()
-        total += r_in[zs]
+    for s in range(1, nz):
+        total += r_in[at(s)]
     gw_v[...] = total
     store_gw = pltpu.make_async_copy(gw_v, gw_o, store_sem.at[4])
     store_gw.start()
 
     for t in range(2):
-        for s in near:
-            hop(t, z, s).wait_send()
-        for source, s in relays:
-            hop(t, at(source), 2 * s, 0 if s > 0 else 1).wait_send()
-            hop(t, at(source), s).wait_send()
-        for zs in range(nz):
-            to_sibling(t, zs).wait_send()
+        hops(t, 0, nz - 1).wait_send()
+        all_siblings(t).wait_send()
         half(t).wait_send()
-        for s in range(1, nz):
-            scatter(t, s).wait_send()
-    for s in range(1, ng):
-        columns_to(s).wait_send()
-        share(s).wait_send()
-    for i in range(yc):
-        for kk in range(2):
-            away, copy = to_y(i, kk)
-            pl.when(away)(copy.wait_send)
-    for s in range(1, nz):
-        to_z(s).wait_send()
+        all_scattered(t).wait_send()
+    all_columns().wait_send()
+    all_shared().wait_send()
+    pl.when(source_core == k)(all_y(2 * yc - 1).wait_send)
+    pl.when(source_core != k)(all_y(2 * yc).wait_send)
+    all_z().wait_send()
 
     for one in (store_ctx, store_gq, store_gv, store_gk, store_gw):
         one.wait()
@@ -467,32 +473,24 @@
             pltpu.VMEM((ng, yc) + sq, bf16),
             pltpu.VMEM((yc, BLOCK, ng * BLOCK), bf16),
             pltpu.VMEM((ng,) + sq, bf16),
-            pltpu.VMEM((yc, 2, nz * fr, BLOCK), bf16),
+            pltpu.VMEM((2 * yc, nz * fr, BLOCK), bf16),
             pltpu.VMEM((ny, nz * fr, BLOCK), bf16),
             pltpu.VMEM((nz * fr, BLOCK), f32),
             pltpu.VMEM((nz, fr, BLOCK), f32),
             pltpu.VMEM((fr, BLOCK), f32),
+            pltpu.SemaphoreType.REGULAR((4,)),
             dma((5,)),
             dma((5,)),
-            dma((2, nz, 5)),
-            dma((2, nz)),
-            dma((2, 2)),
-            dma((2, 2)),
-            dma((2, nz)),
-            dma((2, nz)),
-            dma((2,)),
-            dma((2,)),
-            dma((2, nz)),
-            dma((2, nz)),
-            dma((ng,)),
-            dma((ng,)),
-            dma((ng,)),
-            dma((ng,)),
-            dma((yc, 2)),
-            dma((ny,)),
-            dma((nz,)),
-            dma((nz,)),
-        ],
+            dma((2,)),
+            dma((2, 4)),
+            dma((2,)),
+            dma((2,)),
+            dma((2,)),
+            dma((2,)),
+            dma((2,)),
+            dma((2,)),
+        ]
+        + [dma] * 8,
         compiler_params=pltpu.CompilerParams(
             collective_id=0, has_side_effects=True, vmem_limit_bytes=VMEM_LIMIT
         ),

time: 59.9 us -> 55.5 us (0.927)
  Pallas kernels: 59.1 us -> 54.7 us
    pallas_call x1, Pallas kernels: 57.3 us -> 52.8 us  [body(): pl.pallas_call(functools.partial(kernel, nx, ny, nz, heads), out_shape=(j...]
where the time goes in v3:
time: 55.5 us; the launch traced here: 55.3 us
  Pallas kernels  54.7 us (99%)
  between operations  0.64 us (1%)
    pallas_call x1, Pallas kernels, body(): pl.pallas_call(functools.partial(kernel, nx, ny, nz, heads), out_shape=(j...  52.8 us
    pallas_call x1, Pallas kernels, body(): pl.pallas_call(write_out, out_shape=tuple((jax.ShapeDtypeStruct(one.shape...  1.84 us

profile of v3, /device:TPU:1, one launch (start us, length us, event | category | flops | bytes accessed | tf_op | source)
XLA Modules:
  0.0 55.3 jit_solution(922204088705047771)
XLA Ops:
  0.6 52.8 %attention_core.1 = (bf16[128,1024]{1,0:T(8,128)(2,1)}, bf16[128,1024]{1,0:T(8,128)(2,1)}, bf16[128,128]{1,0:T(8,128)(2,1)}, bf16[128,128]{1,0:T(8,128)(2,1)}, f32[8,128]{1,0:T(8,128)}) custom-call(bf16[128,1024]{1,0:T(8,128)(2,1)} %bitcast.9, bf16[128,128]{1,0:T(8,128)(2,1)} %bitcast.11, bf16[128,4096]{1,0:T(8,128)(2,1)} %bitcast.8, ...), custom_call_target="tpu_custom_call" | custom-call | tf_op jit(solution)/shard_map/attention_core/pallas_call | solution.py:434
  53.5 1.8 %write_out.1 = (bf16[128,1024]{1,0:T(8,128)(2,1)}, bf16[128,1024]{1,0:T(8,128)(2,1)}, bf16[128,128]{1,0:T(8,128)(2,1)}, bf16[128,128]{1,0:T(8,128)(2,1)}, f32[8,128]{1,0:T(8,128)}) custom-call(bf16[128,1024]{1,0:T(8,128)(2,1)} %get-tuple-element.15.refs_0_, bf16[128,1024]{1,0:T(8,128)(2,1)} %get-tuple-element.16.refs_1_, ...), custom_call_target="tpu_custom_call" | custom-call | tf_op jit(solution)/shard_map/write_out/pallas_call | solution.py:501

commit v4 on v3

--- a/solution.py
+++ b/solution.py
@@ -68,8 +68,7 @@
     load_w = load(w_hbm, w_v, 2)
     load_q = load(q_hbm, q_v, 3)
     load_gc = load(gc_hbm, gc_v, 4)
-    for one in (load_k, load_x, load_w, load_q, load_gc):
-        one.start()
+    load_k.start()
 
     barrier = pltpu.get_barrier_semaphore()
 
@@ -82,6 +81,8 @@
     partners = planar + [{"ctx": 2 * lax.rem(z + s, nz) + k} for s in around(nz, 2)]
     for device in partners:
         pl.semaphore_signal(barrier, 1, device_id=device, device_id_type=MESH)
+    for one in (load_q, load_x, load_w, load_gc):
+        one.start()
     pl.semaphore_wait(barrier, len(partners))
 
     def tell(n):
@@ -238,16 +239,20 @@
             sib_out[t, zs] = pad[t, pb + 2 * zs + 1 - k - first]
         half(t).start()
 
-    def scatter(t, s):
+    parts = {0: (slice(0, BLOCK),), 1: (slice(0, BLOCK // 2), slice(BLOCK // 2, BLOCK))}
+
+    def scatter(t, s, n):
+        rows = parts[t][n]
         return remote(
-            rs_out.at[t, at(s)], rs_in.at[t, z], rs_send.at[t], rs_recv.at[t],
+            rs_out.at[t, at(s), rows], rs_in.at[t, z, rows], rs_send.at[t + n], rs_recv.at[t + n],
             {"ctx": 2 * at(s) + k},
         )
 
-    def all_scattered(t):
+    def all_scattered(t, n):
+        many = pl.ds(0, nz - 1)
         return remote(
-            rs_out.at[t, pl.ds(0, nz - 1)], rs_in.at[t, pl.ds(0, nz - 1)],
-            rs_send.at[t], rs_recv.at[t], sibling,
+            rs_out.at[t, many, parts[t][n]], rs_in.at[t, many, parts[t][n]],
+            rs_send.at[t + n], rs_recv.at[t + n], sibling,
         )
 
     def scatter_sums(t):
@@ -257,19 +262,20 @@
                 jnp.float32
             )
             rs_out[t, zs] = both.astype(jnp.bfloat16)
-        for s in sorted(range(1, nz), key=lambda s: -min(s, nz - s)):
-            scatter(t, s).start()
-
-    def gathered(t):
-        all_scattered(t).wait_recv()
-        total = rs_out[t, z].astype(jnp.float32)
+        for n in range(len(parts[t])):
+            for s in sorted(range(1, nz), key=lambda s: -min(s, nz - s)):
+                scatter(t, s, n).start()
+
+    def gathered(t, n):
+        all_scattered(t, n).wait_recv()
+        total = rs_out[t, z, parts[t][n]].astype(jnp.float32)
         for s in range(1, nz):
-            total += rs_in[t, at(s)].astype(jnp.float32)
+            total += rs_in[t, at(s), parts[t][n]].astype(jnp.float32)
         return total.astype(jnp.bfloat16)
 
     swap_halves(1, vacc, 1.0)
+    scatter_sums(1)
     settle(1)
-    scatter_sums(1)
     hear(2)
     tell(3)
 
@@ -306,17 +312,19 @@
     store_ctx.start()
     store_gq.start()
 
-    gvg[g] = gathered(1)
-
-    def share(s):
+    def share(s, n):
         gg, xx, kk, device = group(s)
-        return remote(gvg.at[g], gvg.at[g], gv_send, gv_recv, device)
-
-    def all_shared():
-        return remote(gvg.at[pl.ds(0, ng - 1)], gvg.at[pl.ds(0, ng - 1)], gv_send, gv_recv, sibling)
-
-    for s in range(1, ng):
-        share(s).start()
+        rows = gvg.at[g, parts[1][n]]
+        return remote(rows, rows, gv_send.at[n], gv_recv.at[n], device)
+
+    def all_shared(n):
+        rows = gvg.at[pl.ds(0, ng - 1), parts[1][n]]
+        return remote(rows, rows, gv_send.at[n], gv_recv.at[n], sibling)
+
+    for n in range(2):
+        gvg[g, parts[1][n]] = gathered(1, n)
+        for s in sorted(range(1, ng), key=lambda s: -min(s, ng - s)):
+            share(s, n).start()
     scatter_sums(0)
 
     all_columns().wait_recv()
@@ -328,7 +336,8 @@
 
     store_gv = pltpu.make_async_copy(gvg.at[g], gv_o, store_sem.at[2])
     store_gv.start()
-    all_shared().wait_recv()
+    all_shared(0).wait_recv()
+    all_shared(1).wait_recv()
 
     group_rows = gvg[...].reshape(ng * BLOCK, BLOCK)
     source_core = lax.div(y, yc)
@@ -361,17 +370,16 @@
 
     r_v[...] = jnp.sum(p_in[...].astype(jnp.float32), axis=0)
 
-    def to_z(s):
-        zs = at(s)
-        rows = pl.ds(pl.multiple_of(zs * fr, fr), fr)
+    def to_z(zs):
+        rows = pl.ds(zs * fr, fr)
         return remote(
             r_v.at[rows], r_in.at[z], r_send, r_recv, {"ctx": 2 * zs + k}
         )
 
-    for s in sorted(range(1, nz), key=lambda s: -min(s, nz - s)):
-        to_z(s).start()
-
-    gkv_v[...] = gathered(0)
+    for zs in range(nz):
+        pl.when(zs != z)(to_z(zs).start)
+
+    gkv_v[...] = gathered(0, 0)
     store_gk = pltpu.make_async_copy(gkv_v, gk_o, store_sem.at[3])
     store_gk.start()
 
@@ -392,9 +400,11 @@
         hops(t, 0, nz - 1).wait_send()
         all_siblings(t).wait_send()
         half(t).wait_send()
-        all_scattered(t).wait_send()
+        for n in range(len(parts[t])):
+            all_scattered(t, n).wait_send()
     all_columns().wait_send()
-    all_shared().wait_send()
+    all_shared(0).wait_send()
+    all_shared(1).wait_send()
     pl.when(source_core == k)(all_y(2 * yc - 1).wait_send)
     pl.when(source_core != k)(all_y(2 * yc).wait_send)
     all_z().wait_send()
@@ -487,10 +497,17 @@
             dma((2,)),
             dma((2,)),
             dma((2,)),
-            dma((2,)),
-            dma((2,)),
-        ]
-        + [dma] * 8,
+            dma((3,)),
+            dma((3,)),
+            dma,
+            dma,
+            dma((2,)),
+            dma((2,)),
+            dma,
+            dma,
+            dma,
+            dma,
+        ],
         compiler_params=pltpu.CompilerParams(
             collective_id=0, has_side_effects=True, vmem_limit_bytes=VMEM_LIMIT
         ),

time: 55.5 us -> 53.5 us (0.964)
  Pallas kernels: 54.7 us -> 52.7 us
    pallas_call x1, Pallas kernels: 52.8 us -> 50.9 us  [body(): pl.pallas_call(functools.partial(kernel, nx, ny, nz, heads), out_shape=(j...]
where the time goes in v4:
time: 53.5 us; the launch traced here: 53.4 us
  Pallas kernels  52.7 us (99%)
  between operations  0.64 us (1%)
    pallas_call x1, Pallas kernels, body(): pl.pallas_call(functools.partial(kernel, nx, ny, nz, heads), out_shape=(j...  50.9 us
    pallas_call x1, Pallas kernels, body(): pl.pallas_call(write_out, out_shape=tuple((jax.ShapeDtypeStruct(one.shape...  1.84 us

profile of v4, /device:TPU:1, one launch (start us, length us, event | category | flops | bytes accessed | tf_op | source)
XLA Modules:
  0.0 53.4 jit_solution(3091010094084090406)
XLA Ops:
  0.6 50.9 %attention_core.1 = (bf16[128,1024]{1,0:T(8,128)(2,1)}, bf16[128,1024]{1,0:T(8,128)(2,1)}, bf16[128,128]{1,0:T(8,128)(2,1)}, bf16[128,128]{1,0:T(8,128)(2,1)}, f32[8,128]{1,0:T(8,128)}) custom-call(bf16[128,1024]{1,0:T(8,128)(2,1)} %bitcast.9, bf16[128,128]{1,0:T(8,128)(2,1)} %bitcast.11, bf16[128,4096]{1,0:T(8,128)(2,1)} %bitcast.8, ...), custom_call_target="tpu_custom_call" | custom-call | tf_op jit(solution)/shard_map/attention_core/pallas_call | solution.py:444
  51.5 1.8 %write_out.1 = (bf16[128,1024]{1,0:T(8,128)(2,1)}, bf16[128,1024]{1,0:T(8,128)(2,1)}, bf16[128,128]{1,0:T(8,128)(2,1)}, bf16[128,128]{1,0:T(8,128)(2,1)}, f32[8,128]{1,0:T(8,128)}) custom-call(bf16[128,1024]{1,0:T(8,128)(2,1)} %get-tuple-element.15.refs_0_, bf16[128,1024]{1,0:T(8,128)(2,1)} %get-tuple-element.16.refs_1_, ...), custom_call_target="tpu_custom_call" | custom-call | tf_op jit(solution)/shard_map/write_out/pallas_call | solution.py:518

commit v5 on v4

--- a/solution.py
+++ b/solution.py
@@ -214,20 +214,20 @@
         kw[i * BLOCK : (i + 1) * BLOCK, :] = k_all[first + i]
     log_scale = score_scale * math.log2(math.e)
 
-    def weigh(p, carry):
+    def weigh(p):
         scores = dot(kw[...], qt[p]) + jnp.concatenate([bias[...], bias[...]], axis=1)
         row_max = jnp.max(scores, axis=0, keepdims=True)
         exp_scores = jnp.exp2(scores * log_scale - row_max * log_scale)
-        weights = (exp_scores * (1.0 / jnp.sum(exp_scores, axis=0, keepdims=True))).astype(
-            jnp.bfloat16
-        )
-        wt[p] = weights
-        vacc[...] += dot(weights, gcn[p])
-        return carry
-
-    lax.fori_loop(0, pairs // 2, weigh, 0, unroll=True)
+        wt[:, 2 * BLOCK * p : 2 * BLOCK * (p + 1)] = (
+            exp_scores * (1.0 / jnp.sum(exp_scores, axis=0, keepdims=True))
+        ).astype(jnp.bfloat16)
+
+    for p in range(pairs // 2):
+        weigh(p)
     relay(1)
-    lax.fori_loop(pairs // 2, pairs, weigh, 0, unroll=True)
+    for p in range(pairs // 2, pairs):
+        weigh(p)
+    vacc[...] = dot(wt[...], gcn[...].reshape(heads * BLOCK, BLOCK))
 
     def half(t):
         return remote(sib_out.at[t], sib_in.at[t], half_send.at[t], half_recv.at[t], sibling)
@@ -288,7 +288,7 @@
         vwt[:, i * BLOCK : (i + 1) * BLOCK] = value_block.T
 
     def attend(p, carry):
-        weights = wt[p]
+        weights = wt[:, pl.ds(pl.multiple_of(p * 2 * BLOCK, 2 * BLOCK), 2 * BLOCK)]
         turned = gct[p]
         context = dot(vwt[...], weights).astype(jnp.bfloat16)
         delta = jnp.sum(
@@ -468,7 +468,7 @@
             pltpu.VMEM((span, BLOCK), bf16),
             pltpu.VMEM((BLOCK, span), bf16),
             pltpu.VMEM((BLOCK, span), bf16),
-            pltpu.VMEM((pairs, span, 2 * BLOCK), bf16),
+            pltpu.VMEM((span, heads * BLOCK), bf16),
             pltpu.VMEM((span, BLOCK), f32),
             pltpu.VMEM((span, BLOCK), f32),
             pltpu.VMEM((2, pb + nc) + sq, bf16),

time: 53.5 us -> 53.4 us (level)
  no operation moved by 1% of the time
where the time goes in v5:
time: 53.4 us; the launch traced here: 53.2 us
  Pallas kernels  52.5 us (98%)
  between operations  0.64 us (1%)
    pallas_call x1, Pallas kernels, body(): pl.pallas_call(functools.partial(kernel, nx, ny, nz, heads), out_shape=(j...  50.7 us
    pallas_call x1, Pallas kernels, body(): pl.pallas_call(write_out, out_shape=tuple((jax.ShapeDtypeStruct(one.shape...  1.84 us

profile of v5, /device:TPU:1, one launch (start us, length us, event | category | flops | bytes accessed | tf_op | source)
XLA Modules:
  0.0 53.2 jit_solution(11171840989603801853)
XLA Ops:
  0.6 50.7 %attention_core.1 = (bf16[128,1024]{1,0:T(8,128)(2,1)}, bf16[128,1024]{1,0:T(8,128)(2,1)}, bf16[128,128]{1,0:T(8,128)(2,1)}, bf16[128,128]{1,0:T(8,128)(2,1)}, f32[8,128]{1,0:T(8,128)}) custom-call(bf16[128,1024]{1,0:T(8,128)(2,1)} %bitcast.9, bf16[128,128]{1,0:T(8,128)(2,1)} %bitcast.11, bf16[128,4096]{1,0:T(8,128)(2,1)} %bitcast.8, ...), custom_call_target="tpu_custom_call" | custom-call | tf_op jit(solution)/shard_map/attention_core/pallas_call | solution.py:444
  51.3 1.8 %write_out.1 = (bf16[128,1024]{1,0:T(8,128)(2,1)}, bf16[128,1024]{1,0:T(8,128)(2,1)}, bf16[128,128]{1,0:T(8,128)(2,1)}, bf16[128,128]{1,0:T(8,128)(2,1)}, f32[8,128]{1,0:T(8,128)}) custom-call(bf16[128,1024]{1,0:T(8,128)(2,1)} %get-tuple-element.15.refs_0_, bf16[128,1024]{1,0:T(8,128)(2,1)} %get-tuple-element.16.refs_1_, ...), custom_call_target="tpu_custom_call" | custom-call | tf_op jit(solution)/shard_map/write_out/pallas_call | solution.py:518
